TPU v7x, 256 devices: a whole 4x4x8 slice. The times are simulated.
256 devices in a mesh: pre: 4 (over x_lo, core), main: 64 (over z, x_hi, y).
Axes of the slice: x: 4 (x_hi: 2, x_lo: 2; x = x_hi * 2 + x_lo), y: 4, z: 8, core: 2. Of those that a mesh axis runs over, the one named last changes fastest.
Arguments:
- pre_velocity: float32 [3, 16, 512, 512], P(None, None, 'main', 'pre'), may hold values from -4 to 4
- deck_velocity: float32 [3, 16, 1024, 512], P(None, None, 'main', 'pre'), may hold values from -4 to 4
- deck_force: float32 [16, 1024, 512], P(None, 'main', 'pre'), may hold values from -4 to 4
- inlet_shift: int32 [4], replicated, may hold values from 0 to 511, as said below
- tap_offset: int32 [1024, 4], P('main'), may hold values from -1 to 2
- tap_weight: float32 [1024, 4], P('main'), may hold values from 0.1 to 0.5
- phase_index: int32 [4], replicated, may hold values from 0 to 63
Outputs:
- pre_final: float32 [3, 16, 512, 512], P(None, None, 'main', 'pre')
- deck_final: float32 [3, 16, 1024, 512], P(None, None, 'main', 'pre')
Inputs may be any that keep to these rules, and one draw needn't show every extreme that they name: `inlet_shift`: the shifts of the 4 steps include 0, 256 and 511.
All inputs are finite; a program needn't handle non-finite values.
Results may differ from a plain program's by a relative error of at most 0.00005.
Values sent between devices are 32-bit elements; how exact they have to be, the bound alone decides.
A program may use at most 128 MiB of HBM per device.

v0:
```python
import functools

import jax
import jax.numpy as jnp
from jax import lax
from jax.experimental import pallas as pl
from jax.experimental.pallas import tpu as pltpu
from jax.sharding import PartitionSpec as P

STEPS = 4
SWEEPS = 7
PERIOD = 64
TIME_STEP = 0.2
VISCOSITY = 0.5
DRIVE = 0.05
FORCING = 2.0
TWO_PI = 6.283185307179586

MESH = pl.DeviceIdType.MESH
X = 16
LANES = 128
REACH = SWEEPS + 2
SLOT = 8
WIDTH = 8
BLOCK = 8
NEAR = 8


def padded(depth):
    return -(-depth // SLOT) * SLOT


class Grid:
    def __init__(self, rows, depth, periodic, refs):
        self.n, self.depth, self.periodic = rows, depth, periodic
        self.base = padded(depth)
        self.u, self.v, self.pa, self.pb, self.s = refs

    @staticmethod
    def scratch(rows, depth, periodic, comps):
        total = rows + 2 * padded(depth)
        subs = X if periodic else 32
        field = pltpu.VMEM((2, total, subs, LANES), jnp.float32)
        return [
            pltpu.VMEM((comps, 2, total, subs, LANES), jnp.float32),
            pltpu.VMEM((3, 2, total, subs, LANES), jnp.float32),
            field,
            field,
            pltpu.VMEM((2, total, X, LANES), jnp.float32),
        ]

    def at(self, ref, *index):
        if self.periodic:
            return ref[index]
        return ref[index + (slice(8, 24), slice(None))]

    def xs(self, ref, center, *index):
        if self.periodic:
            return pltpu.roll(center, 1, 0), pltpu.roll(center, X - 1, 0)
        return ref[index + (slice(7, 23), slice(None))], ref[index + (slice(9, 25), slice(None))]

    def put(self, ref, value, *index):
        if self.periodic:
            ref[index] = value
        else:
            ref[index + (slice(8, 24), slice(None))] = value

    def put_high(self, ref, value, *index):
        if not self.periodic:
            ref[index + (slice(24, 25), slice(None))] = value[X - 1 : X]


def loop_rows(low, high, body, width=WIDTH):
    count = (high - low) // width

    def run(k, carry):
        body(low + k * width, width)
        return carry

    if count > 1:
        lax.fori_loop(0, count, run, 0)
    elif count:
        body(low, width)
    if count * width < high - low:
        body(low + count * width, high - low - count * width)


def z_pair(parity, even, odd):
    if parity == 0:
        return pltpu.roll(odd, 1, 1), odd
    return even, pltpu.roll(even, LANES - 1, 1)


def solve(g, depth, spare, masks, force):
    lo, hi = g.base - depth, g.base + g.n + depth

    def provisional(i, width):
        for row in range(width):
            r = i + row
            mid = [[g.at(g.u, c, q, r) for q in range(2)] for c in range(3)]
            for q in range(2):
                less = [1.0 - mid[c][q] for c in range(3)]
                more = [1.0 + mid[c][q] for c in range(3)]
                for c in range(3):
                    u = mid[c][q]
                    xm, xp = g.xs(g.u, u, c, q, r)
                    ym, yp = g.at(g.u, c, q, r - 1), g.at(g.u, c, q, r + 1)
                    zm, zp = z_pair(q, mid[c][0], mid[c][1])
                    around = (less[0] * xp + more[0] * xm) + (less[1] * yp + more[1] * ym)
                    around = around + (less[2] * zp + more[2] * zm)
                    value = (1.0 - 6.0 * TIME_STEP * VISCOSITY) * u + (TIME_STEP * VISCOSITY) * around
                    value = force(value, c, q, r) * masks[q]
                    g.put(g.v, value, c, q, r)
                    if c == 0:
                        g.put_high(g.v, value, c, q, r)

    loop_rows(lo + 1, hi - 1, provisional, 4)

    reach = SWEEPS - 1 + spare
    lo, hi = g.base - reach, g.base + g.n + reach

    def source(i, width):
        for row in range(width):
            r = i + row
            vz = [g.at(g.v, 2, q, r) for q in range(2)]
            for q in range(2):
                xm, xp = g.xs(g.v, g.at(g.v, 0, q, r) if g.periodic else None, 0, q, r)
                zm, zp = z_pair(q, vz[0], vz[1])
                total = (xp - xm) + (g.at(g.v, 1, q, r + 1) - g.at(g.v, 1, q, r - 1)) + (zp - zm)
                value = total * (masks[q] * (0.5 / TIME_STEP / 6.0))
                g.s[q, r] = value
                g.put(g.pa, -value, q, r)

    loop_rows(lo, hi, source)

    sixth = [m * (1.0 / 6.0) for m in masks]
    src, dst = g.pa, g.pb
    for k in range(1, SWEEPS):

        def sweep(i, width, src=src, dst=dst):
            mid = [[g.at(src, q, i + row) for q in range(2)] for row in range(-1, width + 1)]
            for row in range(width):
                for q in range(2):
                    center = mid[row + 1][q]
                    xm, xp = g.xs(src, center, q, i + row)
                    zm, zp = z_pair(q, mid[row + 1][0], mid[row + 1][1])
                    total = ((xm + xp) + (mid[row][q] + mid[row + 2][q])) + (zm + zp)
                    g.put(dst, total * sixth[q] - g.s[q, i + row], q, i + row)

        loop_rows(lo + k, hi - k, sweep)
        src, dst = dst, src


def correct(g, depth, masks):
    scales = [m * (TIME_STEP * 0.5) for m in masks]

    def rows(i, width):
        mid = [[g.at(g.pa, q, i + row) for q in range(2)] for row in range(-1, width + 1)]
        for row in range(width):
            r = i + row
            for q in range(2):
                xm, xp = g.xs(g.pa, mid[row + 1][q], q, r)
                zm, zp = z_pair(q, mid[row + 1][0], mid[row + 1][1])
                slopes = (xp - xm, mid[row + 2][q] - mid[row][q], zp - zm)
                for c in range(3):
                    value = g.at(g.v, c, q, r) - scales[q] * slopes[c]
                    g.put(g.u, value, c, q, r)
                    g.put_high(g.u, value, c, q, r)

    loop_rows(g.base - depth, g.base + g.n + depth, rows, 4)


class Halo:
    def __init__(self, g, comps, depth, refs):
        self.g, self.comps, self.depth = g, comps, depth
        self.rm, self.left, self.right, self.to_left, self.to_right = refs
        self.base = padded(depth)
        self.copies = []

    @staticmethod
    def scratch(rows, depth, comps):
        total = rows + 2 * padded(depth)
        edge = pltpu.VMEM((comps, total // SLOT, X, LANES), jnp.float32)
        own = pltpu.VMEM((comps, rows // SLOT, X, LANES), jnp.float32)
        return [pltpu.VMEM((comps, total, X, LANES), jnp.float32), edge, edge, own, own]

    @staticmethod
    def plan(rows, depth):
        out = []
        for dm in (0, 1, -1, 2, -2, 3, -3):
            first, end = max(0, rows * dm - depth), min(rows, rows * dm + rows + depth)
            if first < end:
                out.append((dm, first, end))
        return out

    def pack(self, lane, c, fetch):
        edges = ((lane >= 32) & (lane < 40)) | ((lane >= 88) & (lane < 96))
        slot_right = lane // 16
        slot_left = lax.rem(lane + 56, LANES) // 16
        for b in range(self.g.n // SLOT):
            lefts = rights = None
            for s in range(SLOT):
                r = b * SLOT + s
                even, odd, merged = fetch(r)
                self.rm[c, self.base + r] = merged
                both = jnp.where(edges, even, pltpu.roll(odd, 8, 1))
                a = pltpu.roll(both, (16 * s + 40) % LANES, 1)
                z = pltpu.roll(both, (16 * s - 88) % LANES, 1)
                lefts = a if s == 0 else jnp.where(slot_left == s, a, lefts)
                rights = z if s == 0 else jnp.where(slot_right == s, z, rights)
            self.to_left[c, b] = lefts
            self.to_right[c, b] = rights

    def send(self, net):
        n, base = self.g.n, self.base
        for dm, first, end in self.plan(n, self.depth):
            start = base + first - n * dm
            if dm:
                net.send(
                    self.rm.at[:, pl.ds(base + first, end - first)],
                    self.rm.at[:, pl.ds(start, end - first)],
                    0,
                    dm,
                    self.copies,
                )
            low, high = first // SLOT, -(-end // SLOT)
            there = base // SLOT + low - n // SLOT * dm
            for dp, mine, theirs in ((-1, self.to_left, self.right), (1, self.to_right, self.left)):
                net.send(
                    mine.at[:, pl.ds(low, high - low)],
                    theirs.at[:, pl.ds(there, high - low)],
                    dp,
                    dm,
                    self.copies,
                )

    def finish(self, lane, c, own, put):
        inner = (lane >= 32) & (lane < 96)
        for r in range(-self.depth, self.g.n + self.depth):
            block, s = (r + self.base) // SLOT, (r + self.base) % SLOT
            mine = (lane >= 16 * s) & (lane < 16 * s + 16)
            outer = jnp.where(mine, self.left[c, block], self.right[c, block])
            kept = own is not None and 0 <= r < self.g.n
            row = None if kept else self.rm[c, r + self.base]
            for q in range(2):
                value = own(q, r) if kept else pltpu.roll(row, 96 if q else 32, 1)
                margin = pltpu.roll(outer, (24 - 8 * q - 16 * s) % LANES, 1)
                put(q, r, jnp.where(inner, value, margin))


class Net:
    def __init__(self, sems_out, sems_in):
        self.out, self.into, self.count, self.all = sems_out, sems_in, 0, []
        self.p, self.m = lax.axis_index("pre"), lax.axis_index("main")
        self.np, self.nm = lax.axis_size("pre"), lax.axis_size("main")

    def device(self, dp, dm):
        return (lax.rem(self.p + dp + self.np, self.np), lax.rem(self.m + dm + self.nm, self.nm))

    def send(self, src, dst, dp, dm, copies):
        copy = pltpu.make_async_remote_copy(
            src_ref=src,
            dst_ref=dst,
            send_sem=self.out.at[self.count],
            recv_sem=self.into.at[self.count],
            device_id=self.device(dp, dm),
            device_id_type=MESH,
        )
        self.count += 1
        copy.start()
        copies.append(copy)
        self.all.append(copy)


PRE_ROWS, DECK_ROWS = 8, 16
DEPTHS = (12, 11, 10, 9)
DEPTH = DEPTHS[0]
ROWS_IN = DECK_ROWS + 2 * 16
WINDOW = 24
FIRST = -7
NEAR_LOW = -(NEAR // 2) + (FIRST // BLOCK)
NEAR_HIGH = NEAR // 2 - 1 + (FIRST + BLOCK - 1 + WINDOW - 1) // BLOCK


def neighbours_of_all(far):
    out = set()
    for rows in (PRE_ROWS, DECK_ROWS):
        for dm, _, _ in Halo.plan(rows, DEPTH):
            out |= {(dp, dm) for dp in (-1, 0, 1)}
    out |= {(0, d) for d in range(NEAR_LOW, NEAR_HIGH + 1)}
    out |= {(0, -d) for d in range(NEAR_LOW, NEAR_HIGH + 1)}
    out |= {(0, NEAR * h) for h in range(-(far // 2) + 1, far // 2 + 1)}
    out.discard((0, 0))
    return sorted(out)


def kernel(far, pre_in, deck_in, force_in, taps_in, shifts, amplitudes, pre_out, deck_out, *scratch):
    scratch = list(scratch)

    def take(count):
        got = scratch[:count]
        del scratch[:count]
        return got

    sems_out, sems_in = take(2)
    pre = Grid(PRE_ROWS, DEPTH, True, take(5))
    deck = Grid(DECK_ROWS, DEPTH, False, take(5))
    pre_halos = [Halo(pre, 1 if t else 3, d, take(5)) for t, d in enumerate((DEPTH,) + DEPTHS[:-1])]
    deck_halos = [Halo(deck, 1 if t else 4, d, take(5)) for t, d in enumerate((DEPTH,) + DEPTHS[:-1])]
    taps, mix = take(2)
    planes = [take(7) for _ in range(STEPS)]
    pre_flat, deck_flat, force_flat = take(3)

    net = Net(sems_out, sems_in)
    barrier = pltpu.get_barrier_semaphore()
    peers = neighbours_of_all(far)
    for dp, dm in peers:
        pl.semaphore_signal(barrier, inc=1, device_id=net.device(dp, dm), device_id_type=MESH)

    lane = lax.broadcasted_iota(jnp.int32, (X, LANES), 1)
    masks = []
    for q in range(2):
        place = net.p * LANES + (lane - 32) * 2 + q
        masks.append(jnp.where((place >= 0) & (place < net.np * LANES), 1.0, 0.0))

    z_of = lax.broadcasted_iota(jnp.int32, (LANES, LANES), 0)
    l_of = lax.broadcasted_iota(jnp.int32, (LANES, LANES), 1)
    sort = jnp.where(z_of == jnp.where(l_of < 64, 2 * l_of, 2 * l_of - 127), 1.0, 0.0)
    unsort = jnp.where(l_of == jnp.where(z_of < 64, 2 * z_of, 2 * z_of - 127), 1.0, 0.0)

    def dot(a, b):
        return jnp.dot(a, b, precision=lax.Precision.HIGHEST, preferred_element_type=jnp.float32)

    def load(halo, source, flat, comps, first):
        n = halo.g.n
        for c in range(comps):
            flat[c] = dot(source[pl.ds(c * X * n, X * n)], sort)

            def fetch(r):
                value = flat[c, pl.ds(r, X, stride=n)]
                return pltpu.roll(value, 32, 1), pltpu.roll(value, 96, 1), value

            halo.pack(lane, first + c, fetch)

    def unload(halo, comps):
        g = halo.g

        def one(c, carry):
            def put(q, r, value):
                value = value * masks[q]
                g.put(g.u, value, c, q, g.base + r)
                g.put_high(g.u, value, c, q, g.base + r)

            halo.finish(lane, c, None, put)
            return carry

        lax.fori_loop(0, comps, one, 0)

    def merge(even, odd, at=lane):
        return jnp.where(at < 64, pltpu.roll(even, 96, 1), pltpu.roll(odd, 32, 1))

    def give_pressure(halo):
        g = halo.g

        def fetch(r):
            even, odd = g.at(g.pa, 0, g.base + r), g.at(g.pa, 1, g.base + r)
            return even, odd, merge(even, odd)

        halo.pack(lane, 0, fetch)
        halo.send(net)

    def take_pressure(halo):
        g = halo.g
        for copy in halo.copies:
            copy.wait_recv()

        def put(q, r, value):
            g.put(g.pa, value * masks[q], q, g.base + r)

        halo.finish(lane, 0, lambda q, r: g.at(g.pa, q, g.base + r), put)
        correct(g, halo.depth - 1, masks)

    load(pre_halos[0], pre_in, pre_flat, 3, 0)
    pl.semaphore_wait(barrier, len(peers))
    pre_halos[0].send(net)
    load(deck_halos[0], deck_in, deck_flat, 3, 0)
    load(deck_halos[0], force_in, force_flat, 1, 3)
    deck_halos[0].send(net)
    tap_copies = []
    taps[pl.ds(16, DECK_ROWS)] = taps_in[...]
    for dm in (1, -1):
        net.send(taps.at[pl.ds(16, 16)], taps.at[pl.ds(16 - 16 * dm, 16)], 0, dm, tap_copies)
    for ref in (deck.pa, deck.pb):
        ref[:, :, 0:8] = jnp.zeros(ref.shape[:2] + (8, LANES), jnp.float32)
        ref[:, :, 24:32] = jnp.zeros(ref.shape[:2] + (8, LANES), jnp.float32)

    def pre_force(value, c, q, r):
        return value + TIME_STEP * DRIVE if c == 0 else value

    def precursor_step(t):
        if t == 0:
            for copy in pre_halos[0].copies:
                copy.wait_recv()
            unload(pre_halos[0], 3)
        else:
            take_pressure(pre_halos[t])
        solve(pre, DEPTHS[t], 1, masks, pre_force)
        if t + 1 < STEPS:
            give_pressure(pre_halos[t + 1])
        correct(pre, 0, masks)
        block, hop = planes[t][:2]
        wide = lane[:BLOCK]
        for c in range(3):
            for r in range(BLOCK):
                both = [pre.u[c, q, pre.base + r, X - 1 : X] for q in range(2)]
                block[c, r : r + 1] = merge(both[0], both[1], lane[:1])
        hop[0] = block[...]
        copies = []
        for h in range(1, far):
            back = -NEAR * h if h <= far // 2 else NEAR * (far - h)
            net.send(block, hop.at[h], 0, back, copies)
        return copies

    def shift_of(t):
        total = BLOCK * net.nm
        moved = lax.rem(shifts[t] + BLOCK * NEAR // 2, total)
        turn = moved // (BLOCK * NEAR)
        return turn, moved - turn * (BLOCK * NEAR) - BLOCK * NEAR // 2

    def near_hop(t, copies):
        hop, near = planes[t][1:3]
        for copy in copies:
            copy.wait_recv()
        turn, _ = shift_of(t)
        mine = pl.ds(-NEAR_LOW * BLOCK, BLOCK)
        near[:, mine] = hop[turn]
        out = []
        for d in range(NEAR_LOW, NEAR_HIGH + 1):
            if d:
                net.send(near.at[:, mine], near.at[:, pl.ds((d - NEAR_LOW) * BLOCK, BLOCK)], 0, -d, out)
        return out

    def make_mix():
        for copy in tap_copies:
            copy.wait_recv()
        row = lax.broadcasted_iota(jnp.int32, (ROWS_IN, LANES), 0)
        col = lax.broadcasted_iota(jnp.int32, (ROWS_IN, LANES), 1)
        ahead = col - (row // 2 - 8 - 1 - FIRST)
        weights = taps[...]
        total = jnp.zeros((ROWS_IN, LANES), jnp.float32)
        for d in range(4):
            total = jnp.where(ahead == d, weights[:, d : d + 1], total)
        mix[...] = total

    tall = lax.broadcasted_iota(jnp.int32, (ROWS_IN, LANES), 1)

    def inlet(t, copies):
        _, _, near, held, edges, from_left, from_right = planes[t]
        for copy in copies:
            copy.wait_recv()
        _, rest = shift_of(t)
        origin = rest + (FIRST - NEAR_LOW * BLOCK)
        left = right = jnp.zeros((ROWS_IN, LANES), jnp.float32)
        weights = mix[...][:, :WINDOW]
        for c in range(3):
            value = dot(weights, near[c, pl.ds(origin, WINDOW)])
            held[c] = value
            low = (tall >= 16 * c) & (tall < 16 * c + 8)
            high = (tall >= 16 * c + 8) & (tall < 16 * c + 16)
            left = jnp.where(low, pltpu.roll(value, 16 * c, 1), left)
            left = jnp.where(high, pltpu.roll(value, (16 * c + 8 - 64) % LANES, 1), left)
            right = jnp.where(low, pltpu.roll(value, (16 * c - 56) % LANES, 1), right)
            right = jnp.where(high, pltpu.roll(value, (16 * c + 8 - 120) % LANES, 1), right)
        edges[0] = left
        edges[1] = right
        out = []
        net.send(edges.at[0], from_right, -1, 0, out)
        net.send(edges.at[1], from_left, 1, 0, out)
        return out

    def ghosts(t, copies):
        _, _, _, held, _, from_left, from_right = planes[t]
        for copy in copies:
            copy.wait_recv()
        depth = DEPTHS[t] - 1
        inner = (tall >= 32) & (tall < 96)
        for q in range(2):
            spots = net.p * LANES + (tall - 32) * 2 + q
            inside = jnp.where((spots >= 0) & (spots < net.np * LANES), 1.0, 0.0)
            for c in range(3):
                value = pltpu.roll(held[c], 96 if q else 32, 1)
                low = pltpu.roll(from_left[...], (24 - 16 * c - 8 * q) % LANES, 1)
                high = pltpu.roll(from_right[...], (96 - 16 * c - 8 * q) % LANES, 1)
                value = jnp.where(inner, value, jnp.where(tall < 64, low, high)) * inside
                for r in range(-depth, DECK_ROWS + depth):
                    line = value[r + 16 : r + 17]
                    deck.u[c, q, deck.base + r, 7:8] = line
                    if c == 0:
                        deck.v[c, q, deck.base + r, 7:8] = line

    def deck_step(t, copies):
        gain = amplitudes[t]

        def deck_force(value, c, q, r):
            return value + gain * deck.at(deck.u, 3, q, r) if c == 2 else value

        ghosts(t, copies)
        last = t + 1 == STEPS
        solve(deck, DEPTHS[t], 1 if last else 0, masks, deck_force)
        if last:
            correct(deck, 0, masks)
        else:
            give_pressure(deck_halos[t + 1])

    far_copies = {0: precursor_step(0)}
    for copy in deck_halos[0].copies:
        copy.wait_recv()
    unload(deck_halos[0], 4)
    make_mix()
    near_copies = {0: near_hop(0, far_copies[0])}
    far_copies[1] = precursor_step(1)
    for t in range(STEPS):
        edge_copies = inlet(t, near_copies[t])
        if t:
            take_pressure(deck_halos[t])
        if t + 1 < STEPS:
            near_copies[t + 1] = near_hop(t + 1, far_copies[t + 1])
        deck_step(t, edge_copies)
        if t + 2 < STEPS:
            far_copies[t + 2] = precursor_step(t + 2)

    def store(g, flat, target):
        for c in range(3):
            for r in range(g.n):
                even, odd = g.at(g.u, c, 0, g.base + r), g.at(g.u, c, 1, g.base + r)
                flat[c, pl.ds(r, X, stride=g.n)] = merge(even, odd)
            target[pl.ds(c * X * g.n, X * g.n)] = dot(flat[c], unsort)

    store(pre, pre_flat, pre_out)
    store(deck, deck_flat, deck_out)
    for copy in net.all:
        copy.wait_send()


def message_count(far):
    count = 0
    for rows in (PRE_ROWS, DECK_ROWS):
        for depth in (DEPTH,) + DEPTHS[:-1]:
            count += 3 * len(Halo.plan(rows, depth))
    return count + 2 + STEPS * (far - 1 + NEAR_HIGH - NEAR_LOW + 2)


def shards(pre_velocity, deck_velocity, deck_force, inlet_shift, tap_offset, tap_weight, phase_index):
    far = lax.axis_size("main") // NEAR
    steps_of = jnp.arange(-1, LANES - 1, dtype=jnp.int32)
    hits = tap_offset[:, :, None] == steps_of
    taps = jnp.sum(jnp.where(hits, tap_weight[:, :, None], 0.0), axis=1)
    amplitude = jnp.sin(TWO_PI * phase_index.astype(jnp.float32) / PERIOD)
    gains = TIME_STEP * FORCING * amplitude

    vmem = pl.BlockSpec(memory_space=pltpu.VMEM)
    smem = pl.BlockSpec(memory_space=pltpu.SMEM)
    messages = message_count(far)
    scratch = [pltpu.SemaphoreType.DMA((messages,)), pltpu.SemaphoreType.DMA((messages,))]
    scratch += Grid.scratch(PRE_ROWS, DEPTH, True, 3)
    scratch += Grid.scratch(DECK_ROWS, DEPTH, False, 4)
    for t, depth in enumerate((DEPTH,) + DEPTHS[:-1]):
        scratch += Halo.scratch(PRE_ROWS, depth, 1 if t else 3)
    for t, depth in enumerate((DEPTH,) + DEPTHS[:-1]):
        scratch += Halo.scratch(DECK_ROWS, depth, 1 if t else 4)
    scratch += [pltpu.VMEM((ROWS_IN, LANES), jnp.float32)] * 2
    for _ in range(STEPS):
        scratch.append(pltpu.VMEM((3, BLOCK, LANES), jnp.float32))
        scratch.append(pltpu.VMEM((far, 3, BLOCK, LANES), jnp.float32))
        scratch.append(pltpu.VMEM((3, (NEAR_HIGH - NEAR_LOW + 1) * BLOCK, LANES), jnp.float32))
        scratch.append(pltpu.VMEM((3, ROWS_IN, LANES), jnp.float32))
        scratch.append(pltpu.VMEM((2, ROWS_IN, LANES), jnp.float32))
        scratch += [pltpu.VMEM((ROWS_IN, LANES), jnp.float32)] * 2
    scratch.append(pltpu.VMEM((3, X * PRE_ROWS, LANES), jnp.float32))
    scratch.append(pltpu.VMEM((3, X * DECK_ROWS, LANES), jnp.float32))
    scratch.append(pltpu.VMEM((1, X * DECK_ROWS, LANES), jnp.float32))

    pre_rows, deck_rows = 3 * X * PRE_ROWS, 3 * X * DECK_ROWS
    pre, deck = pl.pallas_call(
        functools.partial(kernel, far),
        out_shape=(
            jax.ShapeDtypeStruct((pre_rows, LANES), jnp.float32),
            jax.ShapeDtypeStruct((deck_rows, LANES), jnp.float32),
        ),
        in_specs=[vmem, vmem, vmem, vmem, smem, smem],
        out_specs=(vmem, vmem),
        scratch_shapes=scratch,
        compiler_params=pltpu.CompilerParams(
            collective_id=0, has_side_effects=True, vmem_limit_bytes=56 * 1024 * 1024
        ),
    )(
        pre_velocity.reshape(pre_rows, LANES),
        deck_velocity.reshape(deck_rows, LANES),
        deck_force.reshape(X * DECK_ROWS, LANES),
        taps,
        inlet_shift,
        gains,
    )
    return pre.reshape(pre_velocity.shape), deck.reshape(deck_velocity.shape)


def solution(mesh):
    placed = (
        P(None, None, "main", "pre"),
        P(None, None, "main", "pre"),
        P(None, "main", "pre"),
        P(),
        P("main", None),
        P("main", None),
        P(),
    )
    return jax.shard_map(
        shards,
        mesh=mesh,
        in_specs=placed,
        out_specs=(P(None, None, "main", "pre"), P(None, None, "main", "pre")),
        check_vma=False,
    )
```

profile of v0, /device:TPU:1, one launch (start us, length us, event | category | flops | bytes accessed | tf_op | source)
XLA Modules:
  0.0 108.6 jit_solution(2845247875131412187)
XLA Ops:
  0.6 0.0 copy-start.3
  0.6 0.0 copy-start.2
  0.7 0.6 copy-done.3
  1.3 0.0 copy-start.1
  1.3 0.6 sine_multiply_fusion.amplitudes
  1.8 0.0 copy-done.2
  1.9 0.1 copy-done.1
  2.0 0.7 select_reduce_fusion.taps_in
  2.7 103.5 %shard_map.86 = (f32[384,128]{1,0:T(8,128)}, f32[768,128]{1,0:T(8,128)}) custom-call(f32[384,128]{1,0:T(8,128)} %bitcast.8, f32[768,128]{1,0:T(8,128)} %bitcast.5, f32[256,128]{1,0:T(8,128)} %bitcast.9, f32[16,128]{1,0:T(8,128)} %select_reduce_fusion.taps_in, s32[4]{0:T(128)} %shifts.1, f32[4]{0:T(128)} %sine_multiply_fusion.amplitudes), custom_call_target="tpu_custom_call" | custom-call | tf_op jit(solution)/shard_map/pallas_call | solution.py:584
  106.2 0.0 copy-start
  106.2 1.7 %copy.13 = f32[3,16,8,128]{3,2,1,0:T(8,128)} copy(f32[3,16,8,128]{3,2,1,0:T(8,128)} %bitcast.7) | data formatting | bytes 393216
  107.9 0.0 copy-done
  107.9 0.7 copy.14
  (1 shorter events, 0.0 us)
Async XLA Ops:
  0.6 0.7 copy-start.3
  0.6 1.2 %copy-start.2 = (s32[16,4]{0,1:T(4,128)S(1)}, s32[16,4]{0,1:T(4,128)}, u32[]{:S(2)}) copy-start(s32[16,4]{0,1:T(4,128)} %param.11) | copy-start | bytes 772
  1.3 0.7 copy-start.1
  106.2 1.7 %copy-start = (f32[768,128]{1,0:T(8,128)S(1)}, f32[768,128]{1,0:T(8,128)}, u32[]{:S(2)}) copy-start(f32[768,128]{1,0:T(8,128)} %get-tuple-element.5) | copy-start | bytes 1179652
where the time goes:
time: 109 us
  Pallas kernels  104 us (95%)
  local copies, waits for them, and re-layouts  3.18 us (3%)
  other arithmetic  1.24 us (1%)
    pallas_call x1, Pallas kernels, shards(): pl.pallas_call(functools.partial(kernel, far), out_shape=(jax.ShapeDtypeS...  104 us
    unnamed x10, local copies, waits for them, and re-layouts  3.18 us

commit v1 on v0

--- a/solution.py
+++ b/solution.py
@@ -9,6 +9,7 @@
 
 STEPS = 4
 SWEEPS = 7
+TAPS = 4
 PERIOD = 64
 TIME_STEP = 0.2
 VISCOSITY = 0.5
@@ -21,7 +22,7 @@
 LANES = 128
 REACH = SWEEPS + 2
 SLOT = 8
-WIDTH = 8
+WIDTH = 16
 BLOCK = 8
 NEAR = 8
 
@@ -91,7 +92,7 @@
     return even, pltpu.roll(even, LANES - 1, 1)
 
 
-def solve(g, depth, spare, masks, force):
+def solve(g, depth, spare, masks, force, middle=None):
     lo, hi = g.base - depth, g.base + g.n + depth
 
     def provisional(i, width):
@@ -114,7 +115,7 @@
                     if c == 0:
                         g.put_high(g.v, value, c, q, r)
 
-    loop_rows(lo + 1, hi - 1, provisional, 4)
+    loop_rows(lo + 1, hi - 1, provisional, 8)
 
     reach = SWEEPS - 1 + spare
     lo, hi = g.base - reach, g.base + g.n + reach
@@ -131,7 +132,9 @@
                 g.s[q, r] = value
                 g.put(g.pa, -value, q, r)
 
-    loop_rows(lo, hi, source)
+    loop_rows(lo, hi, source, 8)
+    if middle is not None:
+        middle()
 
     sixth = [m * (1.0 / 6.0) for m in masks]
     src, dst = g.pa, g.pb
@@ -167,7 +170,7 @@
                     g.put(g.u, value, c, q, r)
                     g.put_high(g.u, value, c, q, r)
 
-    loop_rows(g.base - depth, g.base + g.n + depth, rows, 4)
+    loop_rows(g.base - depth, g.base + g.n + depth, rows, 8)
 
 
 class Halo:
@@ -294,7 +297,7 @@
     return sorted(out)
 
 
-def kernel(far, pre_in, deck_in, force_in, taps_in, shifts, amplitudes, pre_out, deck_out, *scratch):
+def kernel(far, pre_hbm, deck_hbm, force_hbm, offsets, weights, shifts, phases, pre_out, deck_out, *scratch):
     scratch = list(scratch)
 
     def take(count):
@@ -310,6 +313,7 @@
     taps, mix = take(2)
     planes = [take(7) for _ in range(STEPS)]
     pre_flat, deck_flat, force_flat = take(3)
+    pre_in, deck_in, force_in, sems_load = take(4)
 
     net = Net(sems_out, sems_in)
     barrier = pltpu.get_barrier_semaphore()
@@ -317,6 +321,11 @@
     for dp, dm in peers:
         pl.semaphore_signal(barrier, inc=1, device_id=net.device(dp, dm), device_id_type=MESH)
 
+    loads = []
+    for k, (hbm, here) in enumerate(((pre_hbm, pre_in), (deck_hbm, deck_in), (force_hbm, force_in))):
+        loads.append(pltpu.make_async_copy(hbm, here, sems_load.at[k]))
+        loads[k].start()
+
     lane = lax.broadcasted_iota(jnp.int32, (X, LANES), 1)
     masks = []
     for q in range(2):
@@ -380,14 +389,21 @@
         halo.finish(lane, 0, lambda q, r: g.at(g.pa, q, g.base + r), put)
         correct(g, halo.depth - 1, masks)
 
+    loads[0].wait()
     load(pre_halos[0], pre_in, pre_flat, 3, 0)
     pl.semaphore_wait(barrier, len(peers))
     pre_halos[0].send(net)
+    loads[1].wait()
+    loads[2].wait()
     load(deck_halos[0], deck_in, deck_flat, 3, 0)
     load(deck_halos[0], force_in, force_flat, 1, 3)
     deck_halos[0].send(net)
     tap_copies = []
-    taps[pl.ds(16, DECK_ROWS)] = taps_in[...]
+    own_taps = jnp.zeros((DECK_ROWS, LANES), jnp.float32)
+    for k in range(TAPS):
+        hit = offsets[:, k : k + 1] + 1 == lane
+        own_taps = own_taps + jnp.where(hit, weights[:, k : k + 1], 0.0)
+    taps[pl.ds(16, DECK_ROWS)] = own_taps
     for dm in (1, -1):
         net.send(taps.at[pl.ds(16, 16)], taps.at[pl.ds(16 - 16 * dm, 16)], 0, dm, tap_copies)
     for ref in (deck.pa, deck.pb):
@@ -446,10 +462,10 @@
         row = lax.broadcasted_iota(jnp.int32, (ROWS_IN, LANES), 0)
         col = lax.broadcasted_iota(jnp.int32, (ROWS_IN, LANES), 1)
         ahead = col - (row // 2 - 8 - 1 - FIRST)
-        weights = taps[...]
+        parts = taps[...]
         total = jnp.zeros((ROWS_IN, LANES), jnp.float32)
         for d in range(4):
-            total = jnp.where(ahead == d, weights[:, d : d + 1], total)
+            total = jnp.where(ahead == d, parts[:, d : d + 1], total)
         mix[...] = total
 
     tall = lax.broadcasted_iota(jnp.int32, (ROWS_IN, LANES), 1)
@@ -461,9 +477,9 @@
         _, rest = shift_of(t)
         origin = rest + (FIRST - NEAR_LOW * BLOCK)
         left = right = jnp.zeros((ROWS_IN, LANES), jnp.float32)
-        weights = mix[...][:, :WINDOW]
+        mixing = mix[...][:, :WINDOW]
         for c in range(3):
-            value = dot(weights, near[c, pl.ds(origin, WINDOW)])
+            value = dot(mixing, near[c, pl.ds(origin, WINDOW)])
             held[c] = value
             low = (tall >= 16 * c) & (tall < 16 * c + 8)
             high = (tall >= 16 * c + 8) & (tall < 16 * c + 16)
@@ -499,14 +515,19 @@
                         deck.v[c, q, deck.base + r, 7:8] = line
 
     def deck_step(t, copies):
-        gain = amplitudes[t]
+        angle = TWO_PI * phases[t].astype(jnp.float32) / PERIOD
+        gain = TIME_STEP * FORCING * jnp.sin(jnp.full((X, LANES), angle, jnp.float32))
 
         def deck_force(value, c, q, r):
             return value + gain * deck.at(deck.u, 3, q, r) if c == 2 else value
 
         ghosts(t, copies)
         last = t + 1 == STEPS
-        solve(deck, DEPTHS[t], 1 if last else 0, masks, deck_force)
+
+        def middle():
+            near_copies[t + 1] = near_hop(t + 1, far_copies[t + 1])
+
+        solve(deck, DEPTHS[t], 1 if last else 0, masks, deck_force, None if last else middle)
         if last:
             correct(deck, 0, masks)
         else:
@@ -523,8 +544,6 @@
         edge_copies = inlet(t, near_copies[t])
         if t:
             take_pressure(deck_halos[t])
-        if t + 1 < STEPS:
-            near_copies[t + 1] = near_hop(t + 1, far_copies[t + 1])
         deck_step(t, edge_copies)
         if t + 2 < STEPS:
             far_copies[t + 2] = precursor_step(t + 2)
@@ -552,14 +571,9 @@
 
 def shards(pre_velocity, deck_velocity, deck_force, inlet_shift, tap_offset, tap_weight, phase_index):
     far = lax.axis_size("main") // NEAR
-    steps_of = jnp.arange(-1, LANES - 1, dtype=jnp.int32)
-    hits = tap_offset[:, :, None] == steps_of
-    taps = jnp.sum(jnp.where(hits, tap_weight[:, :, None], 0.0), axis=1)
-    amplitude = jnp.sin(TWO_PI * phase_index.astype(jnp.float32) / PERIOD)
-    gains = TIME_STEP * FORCING * amplitude
-
     vmem = pl.BlockSpec(memory_space=pltpu.VMEM)
     smem = pl.BlockSpec(memory_space=pltpu.SMEM)
+    hbm = pl.BlockSpec(memory_space=pl.ANY)
     messages = message_count(far)
     scratch = [pltpu.SemaphoreType.DMA((messages,)), pltpu.SemaphoreType.DMA((messages,))]
     scratch += Grid.scratch(PRE_ROWS, DEPTH, True, 3)
@@ -579,6 +593,9 @@
     scratch.append(pltpu.VMEM((3, X * PRE_ROWS, LANES), jnp.float32))
     scratch.append(pltpu.VMEM((3, X * DECK_ROWS, LANES), jnp.float32))
     scratch.append(pltpu.VMEM((1, X * DECK_ROWS, LANES), jnp.float32))
+    for rows in (3 * X * PRE_ROWS, 3 * X * DECK_ROWS, X * DECK_ROWS):
+        scratch.append(pltpu.VMEM((rows, LANES), jnp.float32))
+    scratch.append(pltpu.SemaphoreType.DMA((3,)))
 
     pre_rows, deck_rows = 3 * X * PRE_ROWS, 3 * X * DECK_ROWS
     pre, deck = pl.pallas_call(
@@ -587,7 +604,7 @@
             jax.ShapeDtypeStruct((pre_rows, LANES), jnp.float32),
             jax.ShapeDtypeStruct((deck_rows, LANES), jnp.float32),
         ),
-        in_specs=[vmem, vmem, vmem, vmem, smem, smem],
+        in_specs=[hbm, hbm, hbm, vmem, vmem, smem, smem],
         out_specs=(vmem, vmem),
         scratch_shapes=scratch,
         compiler_params=pltpu.CompilerParams(
@@ -597,9 +614,10 @@
         pre_velocity.reshape(pre_rows, LANES),
         deck_velocity.reshape(deck_rows, LANES),
         deck_force.reshape(X * DECK_ROWS, LANES),
-        taps,
+        tap_offset,
+        tap_weight,
         inlet_shift,
-        gains,
+        phase_index,
     )
     return pre.reshape(pre_velocity.shape), deck.reshape(deck_velocity.shape)
 

time: 109 us -> 100 us (0.917)
  Pallas kernels: 104 us -> 94.9 us
  local copies, waits for them, and re-layouts: 3.18 us -> 4.45 us
  other arithmetic: 1.24 us -> 0 us
    pallas_call x1, Pallas kernels: 104 us -> 94.9 us  [shards(): pl.pallas_call(functools.partial(kernel, far), out_shape=(jax.ShapeDtypeS...]
    unnamed x10, local copies, waits for them, and re-layouts: 3.18 us -> 4.45 us
where the time goes in v1:
time: 100 us
  Pallas kernels  94.9 us (95%)
  local copies, waits for them, and re-layouts  4.45 us (4%)
    pallas_call x1, Pallas kernels, shards(): pl.pallas_call(functools.partial(kernel, far), out_shape=(jax.ShapeDtypeS...  94.9 us
    unnamed x10, local copies, waits for them, and re-layouts  4.45 us

profile of v1, /device:TPU:1, one launch (start us, length us, event | category | flops | bytes accessed | tf_op | source)
XLA Modules:
  0.0 100.1 jit_solution(2852781606801249227)
XLA Ops:
  0.6 0.0 copy-start.1
  0.6 0.7 copy-done.1
  1.3 0.0 copy-start.2
  1.3 0.7 copy.9.offsets
  2.0 0.0 copy-done.2
  2.0 0.7 copy.10.weights
  2.7 94.9 %shard_map.86 = (f32[384,128]{1,0:T(8,128)}, f32[768,128]{1,0:T(8,128)}) custom-call(f32[384,128]{1,0:T(8,128)} %bitcast.8, f32[768,128]{1,0:T(8,128)} %bitcast.5, f32[256,128]{1,0:T(8,128)} %bitcast.9, s32[16,4]{1,0:T(8,128)} %copy.9.offsets, f32[16,4]{1,0:T(8,128)} %copy.10.weights, s32[4]{0:T(128)} %shifts.1, s32[4]{0:T(128)} %phases.1), custom_call_target="tpu_custom_call" | custom-call | tf_op jit(solution)/shard_map/pallas_call | solution.py:601
  97.6 0.0 copy-start
  97.6 1.7 %copy.13 = f32[3,16,8,128]{3,2,1,0:T(8,128)} copy(f32[3,16,8,128]{3,2,1,0:T(8,128)} %bitcast.7) | data formatting | bytes 393216
  99.3 0.0 copy-done
  99.3 0.7 copy.14
Async XLA Ops:
  0.6 0.7 copy-start.1
  1.3 0.7 copy-start.2
  97.6 1.7 %copy-start = (f32[768,128]{1,0:T(8,128)S(1)}, f32[768,128]{1,0:T(8,128)}, u32[]{:S(2)}) copy-start(f32[768,128]{1,0:T(8,128)} %get-tuple-element.5) | copy-start | bytes 1179652
